TPU v7x, 128 devices: a whole 4x4x4 slice. The times are simulated.
128 devices in a mesh: row: 8 (over x_lo, y), col: 16 (over x_hi, z, core).
Axes of the slice: x: 4 (x_hi: 2, x_lo: 2; x = x_hi * 2 + x_lo), y: 4, z: 4, core: 2. Of those that a mesh axis runs over, the one named last changes fastest.
Arguments:
- features: bfloat16 [131072, 128], P(('row', 'col')), may hold values from -6 to 6
- weight: bfloat16 [128, 128], replicated, may hold values from -0.5 to 0.5
- cotangent: bfloat16 [131072, 128], P(('row', 'col')), may hold values from -6 to 6
- degree: int32 [131072], P(('row', 'col')), may hold values from 1 to 64
- tile_vals: bfloat16 [8192, 128, 128], P(('row', 'col')), may hold values from -0.25 to 0.25
- tile_rows: int32 [8192], P(('row', 'col')), may hold values from 0 to 7
- tile_cols: int32 [8192], P(('row', 'col')), may hold values from 0 to 7
- tile_live: int32 [8192], P(('row', 'col')), may hold values 0 or 1
- send_index: int32 [1024, 4], P(('row', 'col')), may hold values from 0 to 7
- remote_vals: bfloat16 [4096, 128, 128], P(('row', 'col')), may hold values from -0.5 to 0.5
- remote_rows: int32 [1024, 4], P(('row', 'col')), may hold values from 0 to 7
- remote_live: int32 [1024, 4], P(('row', 'col')), may hold values 0 or 1
Outputs:
- out_z: bfloat16 [131072, 128], P(('row', 'col'))
- grad_x: bfloat16 [131072, 128], P(('row', 'col'))
- grad_w: float32 [128, 128], replicated
Inputs may be any that keep to these rules, and one draw needn't show every extreme that they name: `tile_rows`: tile indices among one device's 1024 // 128 tiles.
All inputs are finite; a program needn't handle non-finite values. No bound on the sum of `tile_live` or of `remote_live` on one device may be relied on, other than what follows from the above.
Results may differ from a plain program's by a relative error of at most 0.0055.
Values may be sent and summed in bfloat16 or wider, within the bound.
A program may use at most 128 MiB of HBM per device.

v0:
```python
import jax
import jax.numpy as jnp
from jax import lax
from jax.experimental import pallas as pl
from jax.experimental.pallas import tpu as pltpu
from jax.sharding import PartitionSpec as P

MESH = pl.DeviceIdType.MESH
BF16 = jnp.bfloat16
F32 = jnp.float32
TILE = 128
BLOCKS = 8
SLOTS = 4
HALF = 4
FIRST = 8
ROW_RELS = [(a, b) for a in range(2) for b in range(4)]
COL_RELS = [(a, b) for a in range(2) for b in range(4)]


def spot():
    row, col = lax.axis_index("row"), lax.axis_index("col")
    return row // 4, row % 4, col // 8, (col // 2) % 4, col % 2


def row_of(rel):
    x_lo, y, _, _, _ = spot()
    return ((x_lo + rel[0]) % 2) * 4 + (y + rel[1]) % 4


def col_of(rel, flip=0):
    _, _, x_hi, z, core = spot()
    return ((x_hi + rel[0]) % 2) * 8 + ((z + rel[1]) % 4) * 2 + (core + flip) % 2


def kernel(
    features_in,
    weight_in,
    cotangent_in,
    degree_in,
    tile_rows_in,
    tile_cols_in,
    tile_live_in,
    send_index_in,
    remote_rows_in,
    remote_live_in,
    tiles_in,
    remotes_in,
    out_z,
    grad_x,
    grad_w,
    features,
    weight,
    cotangent,
    degree,
    tile_rows,
    tile_cols,
    tile_live,
    send_index,
    remote_rows,
    remote_live,
    tiles,
    remotes,
    inv_col,
    pulled,
    cot_t,
    hiddens,
    prod,
    gathered,
    spread,
    outgoing,
    arrived,
    sent_back,
    returned,
    cross_out,
    cross_in,
    sums,
    ring_half,
    ring_full,
    pair_out,
    pair_in,
    wg,
    wg_core,
    wg_part,
    wg_col,
    wg_mine,
    wg_row,
    wg_half,
    wg_other,
    wg_all,
    beside,
    beside_vmem,
    beside_index,
    relayed,
    beside_sum,
    beside_out,
    beside_in,
    turned,
    send_sem,
    recv_sem,
    local_sem,
    *blocks,
):
    row, col = lax.axis_index("row"), lax.axis_index("col")
    _, _, x_hi, z, core = spot()
    copies = []
    arrivals = set()

    def remote(src, dst, target):
        i = len(copies)
        copy = pltpu.make_async_remote_copy(
            src_ref=src,
            dst_ref=dst,
            send_sem=send_sem.at[i],
            recv_sem=recv_sem.at[i],
            device_id=target,
            device_id_type=MESH,
        )
        copies.append(copy)
        copy.start()
        return copy

    def need(*given):
        for copy in given:
            if id(copy) not in arrivals:
                arrivals.add(id(copy))
                copy.wait_recv()

    def to_row(rel):
        return (row_of(rel), col)

    def to_col(rel, flip=0):
        return (row, col_of(rel, flip))

    barrier = pltpu.get_barrier_semaphore()
    peers = [to_col(rel) for rel in ((0, 1), (0, 3), (1, 0))]
    peers += [to_row(rel) for rel in ((0, 1), (0, 3), (0, 2), (1, 0))]
    peers += [to_col((0, 0), 1)]
    for peer in peers:
        pl.semaphore_signal(barrier, inc=1, device_id=peer, device_id_type=MESH)

    loads = []
    for src, dst in (
        (features_in, features),
        (degree_in, degree),
        (cotangent_in, cotangent),
        (weight_in, weight),
        (send_index_in, send_index),
        (tile_rows_in, tile_rows),
        (tile_cols_in, tile_cols),
        (tile_live_in, tile_live),
        (tiles_in, tiles),
        (remote_rows_in, remote_rows),
        (remote_live_in, remote_live),
        (remotes_in, remotes),
    ):
        load = pltpu.make_async_copy(src, dst, local_sem.at[len(loads)])
        load.start()
        loads.append(load)

    def place(rel):
        return rel[0] * 4 + rel[1] % 4

    def block(rel, flip=0):
        return blocks[place(rel) * 2 + flip]

    own = block((0, 0))
    for load in loads[:2]:
        load.wait()
    inv_row = lax.rsqrt(degree[...].astype(F32))
    for b in range(BLOCKS):
        at = pl.ds(b * TILE, TILE)
        across = jnp.broadcast_to(inv_row[b : b + 1, :], (TILE, TILE)).T
        inv_col[at, :] = across
        own[b] = (features[at, :].astype(F32) * across).astype(BF16)

    def mask(hit, live):
        return (hit.astype(jnp.int32) * live).astype(F32)

    def spread_out(marks, lives, store):
        def body(b):
            value = mask(marks[0] == b, lives[0]) * prod[0]
            for j in range(1, SLOTS):
                value += mask(marks[j] == b, lives[j]) * prod[j]
            store(b, value)

        for b in range(BLOCKS):
            body(b)

    def add_to(ref, first=False):
        def store(b, value):
            ref[b] = value if first else ref[b] + value

        return store

    def dense_back(rel, flip):
        base = col_of(rel, flip) * SLOTS
        for j in range(SLOTS):
            prod[j] = jnp.dot(
                pulled[tile_rows[base + j]], tiles[base + j], preferred_element_type=F32
            )
        marks = [tile_cols[base + j] for j in range(SLOTS)]
        lives = [tile_live[base + j] for j in range(SLOTS)]
        return marks, lives

    crossed = {}

    def cross_make(rel):
        def store(b, value):
            cross_out[place(rel), b] = value.astype(BF16)

        spread_out(*dense_back(rel, 1), store)

    def cross_send(rel):
        at = place(rel)
        crossed[rel] = remote(cross_out.at[at], cross_in.at[at], to_col((0, 0), 1))

    def back_cross(rel):
        cross_make(rel)
        cross_send(rel)

    def back_own(rel):
        at = place(rel)
        need(crossed[rel])

        def store(b, value):
            value += cross_in[at, b].astype(F32)
            if rel == (0, 0):
                spread[b] = value
            else:
                sums[at, b] = value.astype(BF16)

        spread_out(*dense_back(rel, 0), store)

    def forward(rel, flip, first=False):
        base = col_of(rel, flip) * SLOTS
        source = block(rel, flip)
        for j in range(SLOTS):
            prod[j] = jnp.dot(
                tiles[base + j], source[tile_cols[base + j]], preferred_element_type=F32
            )
        marks = [tile_rows[base + j] for j in range(SLOTS)]
        lives = [tile_live[base + j] for j in range(SLOTS)]
        spread_out(marks, lives, add_to(gathered, first))

    def remote_forward(rel):
        i, owner = place(rel), row_of(rel)
        for k in range(SLOTS):
            if rel == (1, 0):
                value = beside[beside_index[k, row]]
            elif rel == (0, 0):
                value = outgoing[k]
            else:
                value = arrived[i * SLOTS + k]
            prod[k] = jnp.dot(remotes[owner * SLOTS + k], value, preferred_element_type=F32)
        marks = [remote_rows[k, owner] for k in range(SLOTS)]
        lives = [remote_live[k, owner] for k in range(SLOTS)]
        spread_out(marks, lives, add_to(gathered))

    def remote_back(rel):
        i, owner = place(rel), row_of(rel)
        for k in range(SLOTS):
            value = jnp.dot(
                pulled[remote_rows[k, owner]],
                remotes[owner * SLOTS + k],
                preferred_element_type=F32,
            )
            live = remote_live[k, owner].astype(F32)
            sent_back[i * SLOTS + k] = (value * live).astype(BF16)

    def returned_sum(side, dy, index, store):
        i = place((side, dy))
        source = returned if dy else sent_back
        for k in range(SLOTS):
            prod[k] = source[i * SLOTS + k].astype(F32)
        marks = [index[k, row_of((0, dy))] for k in range(SLOTS)]
        spread_out(marks, [jnp.int32(1)] * SLOTS, store)

    pl.semaphore_wait(barrier, len(peers))

    z_up, z_down, x_far = to_col((0, 1)), to_col((0, 3)), to_col((1, 0))
    x_near = to_row((1, 0))

    def push(rel_src, rel_dst, target, lo, hi):
        span = pl.ds(lo, hi - lo)
        return remote(block(rel_src).at[span], block(rel_dst).at[span], target)

    shared, mixed, turn, ring, row_sent, back_sent = {}, {}, {}, {}, {}, {}

    def share(rel):
        shared[rel] = remote(block(rel), block(rel, 1), to_col((0, 0), 1))

    def mix(dz):
        if FIRST < BLOCKS:
            mixed[dz] = push((0, dz), (1, dz), x_far, FIRST, BLOCKS)

    def mix_done(dz):
        if FIRST < BLOCKS:
            need(mixed[dz])

    def back_mix(dz):
        if FIRST < BLOCKS:
            turn[dz] = remote(
                sums.at[place((1, dz)), pl.ds(FIRST, BLOCKS - FIRST)],
                turned.at[dz - 1],
                x_far,
            )

    def back_mix_add(dz):
        if FIRST < BLOCKS:
            need(turn[dz])
            at = place((0, dz))
            for b in range(FIRST, BLOCKS):
                total = sums[at, b].astype(F32) + turned[dz - 1, b - FIRST].astype(F32)
                sums[at, b] = total.astype(BF16)

    def row_send(side, dy, source):
        row_sent[side, -dy % 4] = remote(
            source.at[pl.ds(dy * SLOTS, SLOTS)],
            arrived.at[pl.ds(place((side, -dy)) * SLOTS, SLOTS)],
            to_row((0, dy)),
        )

    def back_send(side, dy):
        remote_back((side, dy))
        if dy:
            back_sent[side, -dy % 4] = remote(
                sent_back.at[pl.ds(place((side, dy)) * SLOTS, SLOTS)],
                returned.at[pl.ds(place((side, -dy)) * SLOTS, SLOTS)],
                to_row((0, dy)),
            )

    def send_sums(a, dz, side, lo, hi, target):
        span = pl.ds(lo, hi - lo)
        return remote(sums.at[place((a, dz)), span], ring_full.at[a, side, span], target)

    def ring_start(a, mid, top):
        lower, upper = pl.ds(0, mid), pl.ds(mid, top - mid)
        at = place((a, 2))
        ring["up_half", a] = remote(sums.at[at, lower], ring_half.at[a, lower], z_up)
        ring["down_half", a] = remote(sums.at[at, upper], ring_half.at[a, upper], z_down)
        ring["up_early", a] = send_sums(a, 1, 0, mid, top, z_up)
        ring["down_early", a] = send_sums(a, 3, 1, 0, mid, z_down)

    def ring_late(a, mid, top):
        for name, dz, lo, hi, side, target in (
            ("up", 1, 0, mid, 0, z_up),
            ("down", 3, mid, top, 1, z_down),
        ):
            need(ring[name + "_half", a])
            at = place((a, dz))
            for b in range(lo, hi):
                total = sums[at, b].astype(F32) + ring_half[a, b].astype(F32)
                sums[at, b] = total.astype(BF16)
            ring[name + "_late", a] = send_sums(a, dz, side, lo, hi, target)

    def ring_done(a):
        need(*(ring[name, a] for name in ("up_early", "down_early", "up_late", "down_late")))

    mid = FIRST // 2
    up_a = push((0, 0), (0, 3), z_up, 0, HALF)
    down_a = push((0, 0), (0, 1), z_down, HALF, BLOCKS)
    far_a = push((0, 0), (1, 0), x_far, 0, mid)
    far_b = push((0, 0), (1, 0), x_far, mid, FIRST)
    up_b = push((0, 0), (0, 3), z_up, HALF, BLOCKS)
    down_b = push((0, 0), (0, 1), z_down, 0, HALF)
    near = remote(own, beside, x_near)
    index_near = remote(send_index_in, beside_vmem, x_near)
    far_c = push((0, 0), (1, 0), x_far, FIRST, BLOCKS) if FIRST < BLOCKS else far_b
    loads[4].wait()
    for dy in (1, 3, 2, 0):
        for k in range(SLOTS):
            outgoing[dy * SLOTS + k] = own[send_index[k, row_of((0, dy))]]
        if dy:
            row_send(0, dy, outgoing)
    share((0, 0))

    for load in loads[2:4]:
        load.wait()
    for b in range(BLOCKS):
        at = pl.ds(b * TILE, TILE)
        back = lax.dot_general(
            weight[...], cotangent[at, :], (((1,), (1,)), ((), ())), preferred_element_type=F32
        )
        pulled[b] = (back * inv_row[b : b + 1, :]).astype(BF16)
        cot_t[:, at] = cotangent[at, :].T
    for load in loads[5:]:
        load.wait()

    for rel in [(1, 2), (1, 1), (1, 3)]:
        back_cross(rel)
    need(up_a)
    up_c = push((0, 3), (0, 2), z_up, 0, HALF)
    need(down_a)
    down_c = push((0, 1), (0, 2), z_down, HALF, BLOCKS)
    mix(1)
    for dy in (1, 3):
        back_send(1, dy)
    need(far_a)
    far_up_a = push((1, 0), (1, 3), z_up, 0, mid)
    need(far_b)
    far_down_a = push((1, 0), (1, 1), z_down, mid, FIRST)
    far_up_b = push((1, 0), (1, 3), z_up, mid, FIRST)
    far_down_b = push((1, 0), (1, 1), z_down, 0, mid)
    need(up_b)
    mix(3)
    share((0, 3))
    need(down_b)
    share((0, 1))
    need(far_c)
    share((1, 0))
    for dy in (2, 0):
        back_send(1, dy)
    forward((0, 0), 0, True)
    for rel in [(0, 3), (0, 1), (1, 0)]:
        forward(rel, 0)
    need(down_c)
    mix(2)
    need(up_c)
    share((0, 2))
    for rel in [(0, 2), (0, 1), (0, 3)]:
        back_cross(rel)
    need(shared[0, 0])
    forward((0, 0), 1)
    need(far_up_a)
    far_up_c = push((1, 3), (1, 2), z_up, 0, mid)
    need(far_down_a)
    far_down_c = push((1, 1), (1, 2), z_down, mid, FIRST)

    need(index_near)
    load_index = pltpu.make_async_copy(beside_vmem, beside_index, local_sem.at[len(loads)])
    load_index.start()
    need(near)
    load_index.wait()
    for dy in (1, 3, 2):
        for k in range(SLOTS):
            relayed[dy * SLOTS + k] = beside[beside_index[k, row_of((0, dy))]]
        row_send(1, dy, relayed)
    for rel in [(1, 0), (0, 0)]:
        back_cross(rel)
    for rel in [(1, 2), (1, 1), (1, 3)]:
        back_own(rel)
    ring_start(1, mid, FIRST)
    for dz in (2, 1, 3):
        back_mix(dz)
    need(far_up_b)
    mix_done(3)
    share((1, 3))
    need(far_down_b)
    mix_done(1)
    share((1, 1))
    for rel in [(0, 3), (0, 1), (1, 0)]:
        need(shared[rel])
        forward(rel, 1)
    forward((0, 2), 0)
    need(shared[0, 2])
    forward((0, 2), 1)
    for rel in [(0, 0), (1, 0)]:
        remote_forward(rel)
    for dy in (1, 3, 2):
        need(row_sent[0, dy])
        remote_forward((0, dy))
    for rel in [(1, 3), (1, 1)]:
        forward(rel, 0)
    for rel in [(1, 3), (1, 1)]:
        need(shared[rel])
        forward(rel, 1)
    for dy in (0, 1, 3, 2):
        if dy:
            need(back_sent[1, dy])
        returned_sum(1, dy, beside_index, add_to(beside_sum, dy == 0))
    for b in range(BLOCKS):
        beside_out[b] = beside_sum[b].astype(BF16)
    beside_sent = remote(beside_out, beside_in, x_near)
    need(far_up_c, far_down_c)
    mix_done(2)
    share((1, 2))
    forward((1, 2), 0)
    for dy in (1, 3, 2):
        need(row_sent[1, dy])
        remote_forward((1, dy))
    need(shared[1, 2])
    forward((1, 2), 1)

    for b in range(BLOCKS):
        at = pl.ds(b * TILE, TILE)
        hiddens[at, :] = (inv_col[at, :] * gathered[b]).astype(BF16)
    wg[...] = jnp.dot(cot_t[...], hiddens[...], preferred_element_type=F32)
    half = TILE // 2
    part = half // 8
    mine_half = pl.ds(pl.multiple_of(core * half, half), half)
    other_half = pl.ds(pl.multiple_of((1 - core) * half, half), half)
    halves = remote(wg.at[other_half], wg_core, to_col((0, 0), 1))
    here = x_hi * 4 + z

    def chunk(at):
        return pl.ds(pl.multiple_of(at * part, part), part)

    need(halves)
    wg_part[...] = wg[mine_half, :] + wg_core[...]
    col_parts = []
    for rel in COL_RELS[1:]:
        there = col_of(rel) // 2
        col_parts.append(remote(wg_part.at[chunk(there)], wg_col.at[here], to_col(rel)))
    wg_col[here] = wg_part[chunk(here), :]

    ring_late(1, mid, FIRST)
    for rel in [(0, 2), (0, 1), (0, 3)]:
        back_own(rel)
    for dz in (2, 1, 3):
        back_mix_add(dz)
    ring_start(0, HALF, BLOCKS)
    for dy in (1, 3, 2, 0):
        back_send(0, dy)
    need(*col_parts)
    wg_mine[...] = jnp.sum(wg_col[...], axis=0)
    row_parts = []
    for rel in ROW_RELS[1:]:
        row_parts.append(remote(wg_mine, wg_row.at[row], to_row(rel)))
    wg_row[row] = wg_mine[...]

    need(*row_parts)
    wg_half[here] = jnp.sum(wg_row[...], axis=0)
    col_full = []
    for rel in COL_RELS[1:]:
        col_full.append(remote(wg_half.at[here], wg_half.at[here], to_col(rel)))

    back_own((1, 0))
    ring_done(1)
    for b in range(BLOCKS):
        value = sums[place((1, 0)), b].astype(F32)
        if b < FIRST:
            value += ring_full[1, 0, b].astype(F32) + ring_full[1, 1, b].astype(F32)
        pair_out[b] = value.astype(BF16)
    pair = remote(pair_out, pair_in, x_far)
    ring_late(0, HALF, BLOCKS)
    back_own((0, 0))
    need(*col_full)
    full = remote(wg_half, wg_other, to_col((0, 0), 1))
    wg_all[mine_half, :] = wg_half[...].reshape(half, TILE)
    out_z[...] = jnp.dot(hiddens[...], weight[...], preferred_element_type=F32).astype(BF16)
    need(full)
    wg_all[other_half, :] = wg_other[...].reshape(half, TILE)
    grad_w[...] = wg_all[...].T

    for dy in (0, 1, 3, 2):
        if dy:
            need(back_sent[0, dy])
        returned_sum(0, dy, send_index, add_to(spread))
    need(beside_sent)
    ring_done(0)
    need(pair)
    for b in range(BLOCKS):
        value = spread[b] + pair_in[b].astype(F32) + beside_in[b].astype(F32)
        value += ring_full[0, 0, b].astype(F32) + ring_full[0, 1, b].astype(F32)
        value *= inv_row[b : b + 1, :]
        grad_x[pl.ds(b * TILE, TILE), :] = value.T.astype(BF16)
    for copy in copies:
        copy.wait_send()


def on_device(
    features,
    weight,
    cotangent,
    degree,
    tile_vals,
    tile_rows,
    tile_cols,
    tile_live,
    send_index,
    remote_vals,
    remote_rows,
    remote_live,
):
    nodes, width = features.shape
    vmem = pl.BlockSpec(memory_space=pltpu.VMEM)
    hbm = pl.BlockSpec(memory_space=pl.ANY)
    stack = (BLOCKS, TILE, TILE)
    n_copies = 96
    return pl.pallas_call(
        kernel,
        out_shape=(
            jax.ShapeDtypeStruct((nodes, width), BF16),
            jax.ShapeDtypeStruct((nodes, width), BF16),
            jax.ShapeDtypeStruct((TILE, TILE), F32),
        ),
        in_specs=[hbm] * 12,
        out_specs=(vmem, vmem, vmem),
        scratch_shapes=[
            pltpu.VMEM((nodes, width), BF16),
            pltpu.VMEM(weight.shape, BF16),
            pltpu.VMEM((nodes, width), BF16),
            pltpu.VMEM((BLOCKS, TILE), jnp.int32),
        ]
        + [pltpu.SMEM(tile_rows.shape, jnp.int32)] * 3
        + [pltpu.SMEM(send_index.shape[::-1], jnp.int32)] * 3
        + [
            pltpu.VMEM(tile_vals.shape, BF16),
            pltpu.VMEM(remote_vals.shape, BF16),
            pltpu.VMEM((nodes, TILE), F32),
            pltpu.VMEM(stack, BF16),
            pltpu.VMEM((TILE, nodes), BF16),
            pltpu.VMEM((nodes, TILE), BF16),
            pltpu.VMEM((SLOTS, TILE, TILE), F32),
            pltpu.VMEM(stack, F32),
            pltpu.VMEM(stack, F32),
            pltpu.VMEM((32, TILE, TILE), BF16),
            pltpu.VMEM((32, TILE, TILE), BF16),
            pltpu.VMEM((32, TILE, TILE), BF16),
            pltpu.VMEM((32, TILE, TILE), BF16),
            pltpu.VMEM((8,) + stack, BF16),
            pltpu.VMEM((8,) + stack, BF16),
            pltpu.VMEM((8,) + stack, BF16),
            pltpu.VMEM((2,) + stack, BF16),
            pltpu.VMEM((2, 2) + stack, BF16),
            pltpu.VMEM(stack, BF16),
            pltpu.VMEM(stack, BF16),
            pltpu.VMEM((TILE, TILE), F32),
            pltpu.VMEM((TILE // 2, TILE), F32),
            pltpu.VMEM((TILE // 2, TILE), F32),
            pltpu.VMEM((8, 8, TILE), F32),
            pltpu.VMEM((8, TILE), F32),
            pltpu.VMEM((8, 8, TILE), F32),
            pltpu.VMEM((8, 8, TILE), F32),
            pltpu.VMEM((8, 8, TILE), F32),
            pltpu.VMEM((TILE, TILE), F32),
            pltpu.VMEM(stack, BF16),
            pltpu.VMEM(send_index.shape[::-1], jnp.int32),
            pltpu.SMEM(send_index.shape[::-1], jnp.int32),
            pltpu.VMEM((4 * SLOTS, TILE, TILE), BF16),
            pltpu.VMEM(stack, F32),
            pltpu.VMEM(stack, BF16),
            pltpu.VMEM(stack, BF16),
            pltpu.VMEM((3, max(BLOCKS - FIRST, 1), TILE, TILE), BF16),
            pltpu.SemaphoreType.DMA((n_copies,)),
            pltpu.SemaphoreType.DMA((n_copies,)),
            pltpu.SemaphoreType.DMA((13,)),
        ]
        + [pltpu.VMEM(stack, BF16)] * 16,
        compiler_params=pltpu.CompilerParams(
            collective_id=0, has_side_effects=True, vmem_limit_bytes=63 * 2**20
        ),
    )(
        features,
        weight,
        cotangent,
        degree.reshape(BLOCKS, TILE),
        tile_rows,
        tile_cols,
        tile_live,
        send_index.T,
        remote_rows.T,
        remote_live.T,
        tile_vals,
        remote_vals,
    )


def solution(mesh):
    placed = (
        P(("row", "col"), None),
        P(),
        P(("row", "col"), None),
        P(("row", "col")),
        P(("row", "col"), None, None),
        P(("row", "col")),
        P(("row", "col")),
        P(("row", "col")),
        P(("row", "col"), None),
        P(("row", "col"), None, None),
        P(("row", "col"), None),
        P(("row", "col"), None),
    )
    return jax.shard_map(
        on_device,
        mesh=mesh,
        in_specs=placed,
        out_specs=(P(("row", "col"), None), P(("row", "col"), None), P()),
        check_vma=False,
    )
```

profile of v0, /device:TPU:1, one launch (start us, length us, event | category | flops | bytes accessed | tf_op | source)
XLA Modules:
  0.0 57.6 jit_solution(3646702791014494128)
XLA Ops:
  0.6 52.1 %shard_map.139 = (bf16[1024,128]{1,0:T(8,128)(2,1)}, bf16[1024,128]{1,0:T(8,128)(2,1)}, f32[128,128]{1,0:T(8,128)}) custom-call(bf16[1024,128]{1,0:T(8,128)(2,1)} %features_in.1, bf16[128,128]{1,0:T(8,128)(2,1)} %weight_in.1, bf16[1024,128]{1,0:T(8,128)(2,1)} %cotangent_in.1, s32[8,128]{1,0:T(8,128)} %bitcast.4, s32[64]{0:T(128)} %tile_rows_in.1, ...), custom_call_target="tpu_custom_call" | custom-call | tf_op jit(solution)/shard_map/pallas_call | solution.py:580
  52.8 1.7 %copy.18 = bf16[1024,128]{1,0:T(8,128)(2,1)} copy(bf16[1024,128]{1,0:T(8,128)(2,1)} %get-tuple-element.6) | data formatting | bytes 524288
  54.4 1.7 %copy.19 = bf16[1024,128]{1,0:T(8,128)(2,1)} copy(bf16[1024,128]{1,0:T(8,128)(2,1)} %get-tuple-element.7) | data formatting | bytes 524288
  56.1 1.5 %copy.20 = f32[128,128]{1,0:T(8,128)} copy(f32[128,128]{1,0:T(8,128)} %get-tuple-element.8) | data formatting | bytes 131072
where the time goes:
time: 57.8 us; the launch traced here: 57.6 us
  Pallas kernels  52.1 us (90%)
  local copies, waits for them, and re-layouts  4.81 us (8%)
  between operations  0.64 us (1%)
    pallas_call x1, Pallas kernels, on_device(): pl.pallas_call(kernel, out_shape=(jax.ShapeDtypeStruct((nodes, width), BF...  52.1 us
    unnamed x3, local copies, waits for them, and re-layouts  4.81 us

commit v1 on v0

--- a/solution.py
+++ b/solution.py
@@ -45,6 +45,9 @@
     remote_live_in,
     tiles_in,
     remotes_in,
+    out_z_out,
+    grad_x_out,
+    grad_w_out,
     out_z,
     grad_x,
     grad_w,
@@ -511,6 +514,9 @@
     ring_start(0, HALF, BLOCKS)
     for dy in (1, 3, 2, 0):
         back_send(0, dy)
+    out_z[...] = jnp.dot(hiddens[...], weight[...], preferred_element_type=F32).astype(BF16)
+    store_z = pltpu.make_async_copy(out_z, out_z_out, local_sem.at[13])
+    store_z.start()
     need(*col_parts)
     wg_mine[...] = jnp.sum(wg_col[...], axis=0)
     row_parts = []
@@ -537,15 +543,17 @@
     need(*col_full)
     full = remote(wg_half, wg_other, to_col((0, 0), 1))
     wg_all[mine_half, :] = wg_half[...].reshape(half, TILE)
-    out_z[...] = jnp.dot(hiddens[...], weight[...], preferred_element_type=F32).astype(BF16)
     need(full)
     wg_all[other_half, :] = wg_other[...].reshape(half, TILE)
     grad_w[...] = wg_all[...].T
+    store_w = pltpu.make_async_copy(grad_w, grad_w_out, local_sem.at[14])
+    store_w.start()
 
     for dy in (0, 1, 3, 2):
         if dy:
             need(back_sent[0, dy])
         returned_sum(0, dy, send_index, add_to(spread))
+    stores = [store_z, store_w]
     need(beside_sent)
     ring_done(0)
     need(pair)
@@ -554,8 +562,17 @@
         value += ring_full[0, 0, b].astype(F32) + ring_full[0, 1, b].astype(F32)
         value *= inv_row[b : b + 1, :]
         grad_x[pl.ds(b * TILE, TILE), :] = value.T.astype(BF16)
+        if b % HALF == HALF - 1:
+            at = pl.ds((b + 1 - HALF) * TILE, HALF * TILE)
+            store = pltpu.make_async_copy(
+                grad_x.at[at], grad_x_out.at[at], local_sem.at[15 + b // HALF]
+            )
+            store.start()
+            stores.append(store)
     for copy in copies:
         copy.wait_send()
+    for store in stores:
+        store.wait()
 
 
 def on_device(
@@ -573,7 +590,6 @@
     remote_live,
 ):
     nodes, width = features.shape
-    vmem = pl.BlockSpec(memory_space=pltpu.VMEM)
     hbm = pl.BlockSpec(memory_space=pl.ANY)
     stack = (BLOCKS, TILE, TILE)
     n_copies = 96
@@ -585,8 +601,11 @@
             jax.ShapeDtypeStruct((TILE, TILE), F32),
         ),
         in_specs=[hbm] * 12,
-        out_specs=(vmem, vmem, vmem),
+        out_specs=(hbm, hbm, hbm),
         scratch_shapes=[
+            pltpu.VMEM((nodes, width), BF16),
+            pltpu.VMEM((nodes, width), BF16),
+            pltpu.VMEM((TILE, TILE), F32),
             pltpu.VMEM((nodes, width), BF16),
             pltpu.VMEM(weight.shape, BF16),
             pltpu.VMEM((nodes, width), BF16),
@@ -634,7 +653,7 @@
             pltpu.VMEM((3, max(BLOCKS - FIRST, 1), TILE, TILE), BF16),
             pltpu.SemaphoreType.DMA((n_copies,)),
             pltpu.SemaphoreType.DMA((n_copies,)),
-            pltpu.SemaphoreType.DMA((13,)),
+            pltpu.SemaphoreType.DMA((17,)),
         ]
         + [pltpu.VMEM(stack, BF16)] * 16,
         compiler_params=pltpu.CompilerParams(

time: 57.8 us -> 57.5 us (level)
  no operation moved by 1% of the time
where the time goes in v1:
time: 57.5 us; the launch traced here: 57.3 us
  Pallas kernels  51.9 us (90%)
  local copies, waits for them, and re-layouts  4.81 us (8%)
  between operations  0.64 us (1%)
    pallas_call x1, Pallas kernels, on_device(): pl.pallas_call(kernel, out_shape=(jax.ShapeDtypeStruct((nodes, width), BF...  51.9 us
    unnamed x3, local copies, waits for them, and re-layouts  4.81 us

profile of v1, /device:TPU:1, one launch (start us, length us, event | category | flops | bytes accessed | tf_op | source)
XLA Modules:
  0.0 57.3 jit_solution(16694881644321761194)
XLA Ops:
  0.6 51.9 %shard_map.139 = (bf16[1024,128]{1,0:T(8,128)(2,1)}, bf16[1024,128]{1,0:T(8,128)(2,1)}, f32[128,128]{1,0:T(8,128)}) custom-call(bf16[1024,128]{1,0:T(8,128)(2,1)} %features_in.1, bf16[128,128]{1,0:T(8,128)(2,1)} %weight_in.1, bf16[1024,128]{1,0:T(8,128)(2,1)} %cotangent_in.1, s32[8,128]{1,0:T(8,128)} %bitcast.4, s32[64]{0:T(128)} %tile_rows_in.1, ...), custom_call_target="tpu_custom_call" | custom-call | tf_op jit(solution)/shard_map/pallas_call | solution.py:596
  52.5 1.7 %copy.18 = bf16[1024,128]{1,0:T(8,128)(2,1)} copy(bf16[1024,128]{1,0:T(8,128)(2,1)} %get-tuple-element.6) | data formatting | bytes 524288
  54.2 1.7 %copy.19 = bf16[1024,128]{1,0:T(8,128)(2,1)} copy(bf16[1024,128]{1,0:T(8,128)(2,1)} %get-tuple-element.7) | data formatting | bytes 524288
  55.8 1.5 %copy.20 = f32[128,128]{1,0:T(8,128)} copy(f32[128,128]{1,0:T(8,128)} %get-tuple-element.8) | data formatting | bytes 131072
